TPU v7x, 32 devices: a whole 2x2x4 slice. The times are simulated.
32 devices in a mesh: blk: 16 (over z, y, x), row: 2 (over core).
Axes of the slice: x: 2, y: 2, z: 4, core: 2. Of those that a mesh axis runs over, the one named last changes fastest.
Arguments:
- diag_block: float32 [1024, 1024], P('row'), as said below
- panel_rows: float32 [2, 512, 1024], P('row', 'blk'), may hold values from -6 to 6
- row_ids: int32 [4], replicated, may hold values from 0 to 31, as said below
- col_ids: int32 [96], P('blk'), may hold values from -1 to 31, as said below
- block_rows: int32 [96, 8], P('blk'), may hold values from -1 to 31, as said below
- blocks: float32 [96, 8, 256, 256], P('blk', None, 'row'), may hold values from -6 to 6
Outputs:
- factor_rows: float32 [2, 512, 1024], P('row', 'blk')
- new_blocks: float32 [96, 8, 256, 256], P('blk', None, 'row')
Inputs may be any that keep to these rules, and one draw needn't show every extreme that they name: `row_ids`: strictly increasing and distinct; the last is 31. `col_ids`: each of the 32 block columns stands in exactly one slot; an owner's slots s * 6 to s * 6 + 5 hold its columns first, then -1; owners hold 0 to 6 columns, one owner exactly 6. `block_rows`: for a live slot, entry 0 is its own column, live entries rise strictly and are followed only by -1; an empty slot holds -1 only. A column among row_ids stores the block rows of row_ids from itself on, up to 8 of them. `diag_block`: symmetric positive definite.
All inputs are finite; a program needn't handle non-finite values.
Results may differ from a plain program's by a relative error of at most 0.0003.
Values may be sent and summed in bfloat16 or wider, within the bound.
No kernel may reach another device: no remote copies, remote signals or barrier semaphores. Data moves between devices by JAX's collectives and lax.ppermute only.
A program may use at most 128 MiB of HBM per device.

v0:
```python
import functools

import jax
import jax.numpy as jnp
from jax import lax
from jax.experimental import pallas as pl
from jax.experimental.pallas import tpu as pltpu
from jax.sharding import PartitionSpec as P

BLOCK = 128
PANEL = 32
STEP = 8
F32 = jnp.float32
BF16 = jnp.bfloat16
TN = (((0,), (0,)), ((), ()))
NT = (((1,), (1,)), ((), ()))


def halves(value):
    high = value.astype(BF16)
    return high, (value - high.astype(F32)).astype(BF16)


def in_hbm(value):
    return pltpu.with_memory_space_constraint(value, pltpu.HBM)


def in_vmem(value):
    return pltpu.with_memory_space_constraint(value, pltpu.VMEM)


def repeated(ref, *index):
    *lead, row, lanes = index
    return ref[(*lead, pl.ds(row, STEP, stride=0), lanes)]


def eliminate(columns, tiles, scratch_diag, scratch_below, scratch_rows):
    groups = PANEL // STEP
    sublane = lax.broadcasted_iota(jnp.int32, (STEP, BLOCK), 0)
    for s in range(groups):
        first = s * STEP
        for c in range(STEP):
            scratch_diag[s, c] = columns[first + c][s]
        square = [
            [
                repeated(scratch_diag, s, c, k, slice(None)) if k <= c else None
                for c in range(STEP)
            ]
            for k in range(STEP)
        ]
        inverse = []
        for k in range(STEP):
            inverse.append(pl.reciprocal(square[k][k], approx=True))
            for c in range(k + 1, STEP):
                ratio = square[k][c] * inverse[k]
                for d in range(c, STEP):
                    square[c][d] = square[c][d] - ratio * square[k][d]
        ratios = []
        for k in range(STEP):
            now = [None] * groups
            for g in range(s, groups):
                now[g] = columns[first + k][g] * inverse[k]
            now[s] = jnp.where(sublane > k, now[s], 0.0)
            for c in range(k + 1, STEP):
                for g in range(s, groups):
                    columns[first + c][g] = columns[first + c][g] - now[g] * square[k][c]
            ratios.append(now)
            for g in range(s + 1, groups):
                scratch_below[s, k, (g - 1) * STEP : g * STEP, :] = columns[first + k][g]
        for c in range(first + STEP, PANEL):
            for k in range(STEP):
                entry = repeated(scratch_below, s, k, c - STEP, slice(None))
                for g in range(c // STEP, groups):
                    columns[c][g] = columns[c][g] - ratios[k][g] * entry
        pivots = square[0][0]
        for k in range(1, STEP):
            pivots = jnp.where(sublane == k, square[k][k], pivots)
        for t in range(len(tiles[s])):
            for k in range(STEP):
                scratch_rows[s, t, k % 2] = tiles[s][t]
                row = repeated(scratch_rows, s, t, k % 2, k, slice(None))
                for g in range(s, groups):
                    if g == s and k == STEP - 1:
                        continue
                    tiles[g][t] = tiles[g][t] - ratios[k][g] * row
        scale = lax.rsqrt(pivots)
        tiles[s] = [tile * scale for tile in tiles[s]]


def times_transposed(high, low, right_high, right_low):
    width = right_high.shape[0]
    both = lax.dot_general(
        high, jnp.concatenate([right_high, right_low], axis=0), NT, preferred_element_type=F32
    )
    return (
        both[:, :width]
        + both[:, width:]
        + lax.dot_general(low, right_high, NT, preferred_element_type=F32)
    )


def invert_diagonal(diag, unit, scratch_diag, scratch_below, scratch_rows):
    groups = range(PANEL // STEP)
    for q in range(BLOCK // PANEL):
        top = q * PANEL
        rest = top + PANEL
        tile = diag[top:rest, :]
        columns = [
            [
                jnp.broadcast_to(
                    tile[g * STEP : (g + 1) * STEP, top + c : top + c + 1], (STEP, BLOCK)
                )
                if g >= c // STEP
                else None
                for g in groups
            ]
            for c in range(PANEL)
        ]
        cuts = [slice(top + g * STEP, top + (g + 1) * STEP) for g in groups]
        tiles = [[diag[cut, :], unit[cut, :]] for cut in cuts]
        eliminate(columns, tiles, scratch_diag, scratch_below, scratch_rows)
        for g, cut in enumerate(cuts):
            diag[cut, :] = tiles[g][0]
            unit[cut, :] = tiles[g][1]
        if rest < BLOCK:
            left_high, left_low = halves(diag[top:rest, :])
            left = jnp.concatenate([left_high, left_low, left_high], axis=0)
            for target in (diag, unit):
                right_high, right_low = halves(target[top:rest, :])
                right = jnp.concatenate([right_high, right_high, right_low], axis=0)
                change = lax.dot_general(left, right, TN, preferred_element_type=F32)
                target[rest:, :] = target[rest:, :] - change[rest:, :]


def factor_kernel(first, last, core_ref, own_ref, other_ref, *refs):
    refs = list(refs)
    state_refs = [refs.pop(0) for _ in range(6)] if first else []
    blocks_ref = refs.pop(0) if first else None
    high_ref, low_ref, base, prev_high, prev_low, diag = refs[:6]
    refs = refs[6:]
    copied_ref = refs.pop(0) if first else None
    matrix, unit, scratch_diag, scratch_below, scratch_rows, tile_sems = refs[:6]
    order = own_ref.shape[1]
    half = order // 2
    count = order // BLOCK
    width = high_ref.shape[1]
    core = core_ref[0]

    def fetch_tile(t, which):
        lanes = pl.ds(pl.multiple_of(t * BLOCK, BLOCK), BLOCK)
        source = (own_ref, other_ref)[which]
        at = pl.multiple_of((core if which == 0 else 1 - core) * half, half)
        return pltpu.make_async_copy(
            source.at[:, lanes], matrix.at[t, pl.ds(at, half), :], tile_sems.at[t, which]
        )

    for t in range(first, min(last + 1, count)):
        for which in range(2):
            fetch_tile(t, which).start()
    if first:
        held, block_sems = refs[6:]
        fetch_blocks = pltpu.make_async_copy(blocks_ref, held, block_sems.at[0])
        store_blocks = pltpu.make_async_copy(held, copied_ref, block_sems.at[1])
        fetch_blocks.start()
    identity = (
        lax.broadcasted_iota(jnp.int32, (BLOCK, BLOCK), 0)
        == lax.broadcasted_iota(jnp.int32, (BLOCK, BLOCK), 1)
    ).astype(F32)
    row_at = lax.broadcasted_iota(jnp.int32, (order, BLOCK), 0)

    if first:
        done = (first - 1) * BLOCK
        high_ref[:, done:] = jnp.zeros((order, width - done), BF16)
        low_ref[:, done:] = jnp.zeros((order, width - done), BF16)
        high_ref[:, :done] = state_refs[0][...]
        low_ref[:, :done] = state_refs[1][...]
        for into, out_of in zip((base, prev_high, prev_low, diag), state_refs[2:]):
            into[...] = out_of[...]
        for which in range(2):
            fetch_tile(first, which).wait()
    else:
        for ref in (high_ref, low_ref, base, prev_high, prev_low):
            ref[...] = jnp.zeros(ref.shape, ref.dtype)
        for which in range(2):
            fetch_tile(0, which).wait()
        diag[...] = matrix[0, :BLOCK, :]

    def store_previous(b):
        before = pl.multiple_of(jnp.maximum(b - 1, 0) * BLOCK, BLOCK)
        high_ref[pl.ds(before, BLOCK), :] = jnp.zeros((BLOCK, width), BF16)
        low_ref[pl.ds(before, BLOCK), :] = jnp.zeros((BLOCK, width), BF16)
        column = times_transposed(*halves(base[...]), prev_high[...], prev_low[...])
        high, low = halves(column)
        high_ref[:, pl.ds(before, BLOCK)] = high
        low_ref[:, pl.ds(before, BLOCK)] = low

    def block_step(b, carry):
        here = pl.multiple_of(b * BLOCK, BLOCK)
        following = jnp.minimum(b + 1, count - 1)
        next_at = pl.multiple_of(following * BLOCK, BLOCK)

        @pl.when(b + 1 < count)
        def _():
            for which in range(2):
                fetch_tile(b + 1, which).wait()

        if first:

            @pl.when(b == first + 1)
            def _():
                fetch_blocks.wait()
                store_blocks.start()

        store_previous(b)
        earlier = times_transposed(
            high_ref[...],
            low_ref[...],
            high_ref[pl.ds(here, BLOCK), :],
            low_ref[pl.ds(here, BLOCK), :],
        )
        base[...] = jnp.where(row_at >= here, matrix[b], 0.0) - earlier
        base[pl.ds(here, BLOCK), :] = identity
        next_high, next_low = high_ref[pl.ds(next_at, BLOCK), :], low_ref[pl.ds(next_at, BLOCK), :]
        next_diag = matrix[following, pl.ds(next_at, BLOCK), :] - times_transposed(
            next_high, next_low, next_high, next_low
        )

        unit[...] = identity
        invert_diagonal(diag, unit, scratch_diag, scratch_below, scratch_rows)

        high, low = halves(unit[...])
        prev_high[...] = high
        prev_low[...] = low
        below = times_transposed(*halves(base[pl.ds(next_at, BLOCK), :]), high, low)
        high, low = halves(below)
        diag[...] = next_diag - times_transposed(high, low, high, low)
        return carry

    lax.fori_loop(first, last, block_step, 0)
    if last == count:
        store_previous(count)
    if first:
        store_blocks.wait()


def factor(first, last, core, own, other, state, blocks):
    order = own.shape[1]
    count = order // BLOCK
    vmem = pl.BlockSpec(memory_space=pltpu.VMEM)
    hbm = pl.BlockSpec(memory_space=pltpu.HBM)
    columns = (last if last == count else last - 1) * BLOCK
    out_shape = [
        pltpu.VMEM((order, columns), BF16),
        pltpu.VMEM((order, columns), BF16),
        pltpu.VMEM((order, BLOCK), F32),
        pltpu.VMEM((BLOCK, BLOCK), BF16),
        pltpu.VMEM((BLOCK, BLOCK), BF16),
        pltpu.VMEM((BLOCK, BLOCK), F32),
    ]
    scratch = [
        pltpu.VMEM((count, order, BLOCK), F32),
        pltpu.VMEM((BLOCK, BLOCK), F32),
        pltpu.VMEM((PANEL // STEP, STEP, STEP, BLOCK), F32),
        pltpu.VMEM((PANEL // STEP, STEP, PANEL - STEP, BLOCK), F32),
        pltpu.VMEM((PANEL // STEP, 2, 2, STEP, BLOCK), F32),
        pltpu.SemaphoreType.DMA((count, 2)),
    ]
    in_specs = [pl.BlockSpec(memory_space=pltpu.SMEM), hbm, vmem]
    out_specs = [vmem] * len(out_shape)
    operands = [core, in_hbm(own), in_vmem(other)]
    limit = 12 * 1024 * 1024
    if first:
        in_specs += [vmem] * len(state) + [hbm]
        operands += [in_vmem(part) for part in state] + [in_hbm(blocks)]
        out_specs.append(hbm)
        out_shape.append(jax.ShapeDtypeStruct(blocks.shape, F32))
        scratch += [pltpu.VMEM(blocks.shape, F32), pltpu.SemaphoreType.DMA((2,))]
        limit += 4 * blocks.size + 4 * 1024 * 1024
    share = last - first
    return pl.pallas_call(
        functools.partial(factor_kernel, first, last),
        out_shape=out_shape,
        in_specs=in_specs,
        out_specs=out_specs,
        scratch_shapes=scratch,
        compiler_params=pltpu.CompilerParams(vmem_limit_bytes=limit),
        cost_estimate=pl.CostEstimate(
            flops=share * order**3, bytes_accessed=share * 20_000_000, transcendentals=0
        ),
        name="factor",
    )(*operands)


def solve_kernel(blk_ref, high_ref, low_ref, *refs):
    *piece_refs, own_ref, rounded_ref, rows, rows_high, rows_low, solved, row_sem = refs
    blk = blk_ref[0]
    held, part, order = piece_refs[0].shape
    n_blk = len(piece_refs) * held
    chunk_rows = rows_high.shape[0]
    chunk = chunk_rows // part
    chunks = n_blk // chunk

    def load(at):
        return pltpu.make_async_copy(piece_refs[0].at[pl.ds(at * chunk, chunk)], rows, row_sem)

    def solve_chunk(at, carry):
        if len(piece_refs) == 1:
            load(at).start()
            load(at).wait()
            rows_high[...], rows_low[...] = halves(rows[...].reshape(chunk_rows, order))
        else:
            for k, piece in enumerate(piece_refs):
                for j in range(held):
                    place = blk ^ (k + j * len(piece_refs))
                    here = pl.ds(pl.multiple_of(place * part, part), part)
                    rows_high[here, :], rows_low[here, :] = halves(piece[j])

        width = 256
        for n in range(order // width):
            cut = slice(n * width, (n + 1) * width)
            deep = (n + 1) * width
            x = jnp.dot(
                rows_high[:, :deep], high_ref[:deep, cut], preferred_element_type=F32
            )
            x += jnp.dot(rows_low[:, :deep], high_ref[:deep, cut], preferred_element_type=F32)
            x += jnp.dot(rows_high[:, :deep], low_ref[:deep, cut], preferred_element_type=F32)
            solved[:, cut] = x
            rounded_ref[pl.ds(pl.multiple_of(at * chunk_rows, chunk_rows), chunk_rows), cut] = (
                x.astype(BF16)
            )

        @pl.when(blk // chunk == at)
        def _():
            own_ref[...] = solved[pl.ds(pl.multiple_of(blk % chunk * part, part), part), :]

        return carry

    lax.fori_loop(0, chunks, solve_chunk, 0)


def solve(blk, high, low, pieces):
    order = high.shape[0]
    held, part, _ = pieces[0].shape
    n_blk = len(pieces) * held
    chunk = n_blk if len(pieces) > 1 else min(n_blk, max(1, 512 // part))
    smem = pl.BlockSpec(memory_space=pltpu.SMEM)
    vmem = pl.BlockSpec(memory_space=pltpu.VMEM)
    if len(pieces) > 1:
        piece_spec, row_shape = vmem, (1, 8, BLOCK)
        pieces = [in_vmem(piece) for piece in pieces]
    else:
        piece_spec, row_shape = pl.BlockSpec(memory_space=pltpu.HBM), (chunk, part, order)
        pieces = [in_hbm(piece) for piece in pieces]
    return pl.pallas_call(
        solve_kernel,
        out_shape=[
            jax.ShapeDtypeStruct((part, order), F32),
            pltpu.VMEM((n_blk * part, order), BF16),
        ],
        in_specs=[smem, vmem, vmem] + [piece_spec] * len(pieces),
        out_specs=[vmem, vmem],
        scratch_shapes=[
            pltpu.VMEM(row_shape, F32),
            pltpu.VMEM((chunk * part, order), BF16),
            pltpu.VMEM((chunk * part, order), BF16),
            pltpu.VMEM((chunk * part, order), F32),
            pltpu.SemaphoreType.DMA,
        ],
        compiler_params=pltpu.CompilerParams(vmem_limit_bytes=20 * 1024 * 1024),
        name="solve",
    )(blk, in_vmem(high), in_vmem(low), *pieces)


def pack_kernel(count, *refs):
    out_ref = refs[-1]
    for j in range(count):
        out_ref[j] = refs[j][0]


def pack(parts, after):
    vmem = pl.BlockSpec(memory_space=pltpu.VMEM)
    return pl.pallas_call(
        functools.partial(pack_kernel, len(parts)),
        out_shape=pltpu.VMEM((len(parts),) + parts[0].shape[1:], parts[0].dtype),
        in_specs=[vmem] * (len(parts) + len(after)),
        out_specs=vmem,
        name="pack",
    )(*[in_vmem(value) for value in list(parts) + list(after)])


def update_kernel(
    core_ref, row_ids_ref, col_ids_ref, block_rows_ref,
    mine_ref, theirs_ref, blocks_ref, copied_ref, out_ref,
    held, found, in_sems, out_sems,
):
    del copied_ref
    core = core_ref[0]
    slots, stored = block_rows_ref.shape
    pieces = row_ids_ref.shape[0]
    half_rows = blocks_ref.shape[2]

    def fetch(n, slot, r):
        return pltpu.make_async_copy(blocks_ref.at[slot, r], held.at[n], in_sems.at[n])

    def place_of(wanted):
        def look(p, at):
            return jnp.where(row_ids_ref[p] == wanted, p, at)

        return jnp.where(wanted >= 0, lax.fori_loop(0, pieces, look, jnp.int32(-1)), -1)

    def scan_slot(slot, n):
        a = place_of(col_ids_ref[slot])

        def scan_stored(r, n):
            b = jnp.where(a >= 0, place_of(block_rows_ref[slot, r]), -1)

            @pl.when(b >= 0)
            def _():
                found[0, n] = slot
                found[1, n] = r
                found[2, n] = a
                found[3, n] = b
                fetch(n, slot, r).start()

            return jnp.where(b >= 0, n + 1, n)

        return lax.fori_loop(0, jnp.where(a >= 0, stored, 0), scan_stored, n)

    total = lax.fori_loop(0, slots, scan_slot, jnp.int32(0))

    def store(n):
        return pltpu.make_async_copy(
            held.at[n], out_ref.at[found[0, n], found[1, n]], out_sems.at[n]
        )

    def apply(n, carry):
        a_rows = pl.ds(pl.multiple_of(found[2, n] * half_rows, half_rows), half_rows)
        b_rows = pl.ds(pl.multiple_of(found[3, n] * half_rows, half_rows), half_rows)
        row = mine_ref[b_rows, :]
        column = jnp.concatenate([mine_ref[a_rows, :], theirs_ref[a_rows, :]], axis=0)
        change = lax.dot_general(row, column, NT, preferred_element_type=F32)
        fetch(n, found[0, n], found[1, n]).wait()
        for which in range(2):
            at = (core if which == 0 else 1 - core) * half_rows
            lanes = pl.ds(pl.multiple_of(at, half_rows), half_rows)
            part = change[:, which * half_rows : (which + 1) * half_rows]
            held[n, :, lanes] = held[n, :, lanes] - part
        store(n).start()
        return carry

    lax.fori_loop(0, total, apply, 0)

    def finish(n, carry):
        store(n).wait()
        return carry

    lax.fori_loop(0, total, finish, 0)


def update(core, row_ids, col_ids, block_rows, mine, theirs, blocks, copied):
    slots, stored = block_rows.shape
    smem = pl.BlockSpec(memory_space=pltpu.SMEM)
    vmem = pl.BlockSpec(memory_space=pltpu.VMEM)
    hbm = pl.BlockSpec(memory_space=pltpu.HBM)
    return pl.pallas_call(
        update_kernel,
        out_shape=jax.ShapeDtypeStruct(blocks.shape, F32),
        in_specs=[smem, smem, smem, smem, vmem, vmem, hbm, hbm],
        out_specs=hbm,
        input_output_aliases={7: 0},
        scratch_shapes=[
            pltpu.VMEM((slots * stored,) + blocks.shape[2:], F32),
            pltpu.SMEM((4, slots * stored), jnp.int32),
            pltpu.SemaphoreType.DMA((slots * stored,)),
            pltpu.SemaphoreType.DMA((slots * stored,)),
        ],
        compiler_params=pltpu.CompilerParams(
            vmem_limit_bytes=8 * 1024 * 1024 + 4 * blocks.size + 4 * mine.size
        ),
        name="update",
    )(
        core, row_ids, col_ids, block_rows, in_vmem(mine), in_vmem(theirs),
        in_hbm(blocks), in_hbm(copied),
    )


def local(diag_block, panel_rows, row_ids, col_ids, block_rows, blocks):
    blk = lax.axis_index("blk").astype(jnp.int32)[None]
    core = lax.axis_index("row").astype(jnp.int32)[None]
    swap = [(0, 1), (1, 0)]
    n_blk = lax.axis_size("blk")
    count = diag_block.shape[1] // BLOCK
    other = lax.ppermute(diag_block, "row", swap)

    def from_partner(value, k):
        return lax.ppermute(value, "blk", [(i, i ^ k) for i in range(n_blk)])

    in_stages = n_blk in (8, 16)
    near = n_blk // 4
    if in_stages:
        arrived = [from_partner(panel_rows, j * near) for j in range(1, 4)]
    else:
        pieces = [lax.all_gather(panel_rows, "blk", axis=0, tiled=True)]
    state = factor(0, 2, core, diag_block, other, [], blocks)
    if in_stages:
        group = pack([panel_rows] + arrived, state)
        pieces = [group] + [from_partner(group, k) for k in range(1, near)]
    high, low, *_, copied = factor(2, count, core, diag_block, other, state, blocks)
    own, mine = solve(blk, high, low, pieces)
    theirs = lax.ppermute(mine, "row", swap)
    new_blocks = update(core, row_ids, col_ids, block_rows, mine, theirs, blocks, copied)
    return own[None], new_blocks


def solution(mesh):
    return jax.shard_map(
        local,
        mesh=mesh,
        in_specs=(
            P("row", None),
            P("row", "blk", None),
            P(),
            P("blk"),
            P("blk", None),
            P("blk", None, "row", None),
        ),
        out_specs=(P("row", "blk", None), P("blk", None, "row", None)),
        check_vma=False,
    )
```

profile of v0, /device:TPU:23, one launch (start us, length us, event | category | flops | bytes accessed | tf_op | source)
XLA Modules:
  0.0 65.2 jit_solution(17684395382719869800)
XLA Ops:
  0.6 0.7 %collective-permute-start = (f32[512,1024]{1,0:T(8,128)}, f32[512,1024]{1,0:T(8,128)}, u32[]{:S(2)}, u32[]{:S(2)}) collective-permute-start(f32[512,1024]{1,0:T(8,128)} %own_ref.3), channel_id=1, source_target_pairs={{0,1},{1,0},{2,3},{3,2},{4,5},{5,4},{6,7},{7,6},{8,9},{9,8},{10,11... | collective-permute-start | bytes 6291464 | tf_op jit(solution)/shard_map/ppermute | solution.py:493
  1.4 1.3 %collective-permute-start.1 = (f32[1,32,1024]{2,1,0:T(8,128)}, f32[1,32,1024]{2,1,0:T(8,128)S(1)}, u32[]{:S(2)}, u32[]{:S(2)}) collective-permute-start(f32[1,32,1024]{2,1,0:T(8,128)} %refs_0_.1), channel_id=1, source_target_pairs={{0,8},{2,10},{4,12},{6,14},{8,0},{10,2},{12,4},{14,6},{16,24},{18,... | collective-permute-start | bytes 393224 | tf_op jit(solution)/shard_map/ppermute | solution.py:496
  2.7 0.1 collective-permute-start.2
  2.7 1.3 %collective-permute-start.3 = (f32[1,32,1024]{2,1,0:T(8,128)}, f32[1,32,1024]{2,1,0:T(8,128)S(1)}, u32[]{:S(2)}, u32[]{:S(2)}) collective-permute-start(f32[1,32,1024]{2,1,0:T(8,128)} %refs_0_.1), channel_id=1, source_target_pairs={{0,24},{2,26},{4,28},{6,30},{8,16},{10,18},{12,20},{14,22},{16,8},... | collective-permute-start | bytes 393224 | tf_op jit(solution)/shard_map/ppermute | solution.py:496
  4.0 1.5 %collective-permute-done.other_ref = f32[512,1024]{1,0:T(8,128)} collective-permute-done((f32[512,1024]{1,0:T(8,128)}, f32[512,1024]{1,0:T(8,128)}, u32[]{:S(2)}, u32[]{:S(2)}) %collective-permute-start) | collective-permute-done | bytes 2097184 | tf_op jit(solution)/shard_map/ppermute | solution.py:493
  5.5 0.0 copy-start
  5.5 10.2 %factor.2 = (bf16[1024,128]{1,0:T(8,128)(2,1)S(1)}, bf16[1024,128]{1,0:T(8,128)(2,1)S(1)}, f32[1024,128]{1,0:T(8,128)S(1)}, bf16[128,128]{1,0:T(8,128)(2,1)S(1)}...) custom-call(s32[1]{0:T(128)} %bitcast.1.core_ref, f32[512,1024]{1,0:T(8,128)} %own_ref.3, ...), custom_call_target="tpu_custom_call" | custom-call | flops 2147483648 | bytes 40000000 | tf_op jit(solution)/shard_map/factor/pallas_call | solution.py:280
  15.7 0.0 collective-permute-done.1.refs_1_
  15.7 0.0 collective-permute-done.2.refs_2_
  15.7 0.2 collective-permute-done.3.refs_3_
  16.0 0.0 copy-done
  16.0 0.3 collective-permute-start.4
  16.3 0.2 collective-permute-start.5
  16.6 2.2 %collective-permute-start.6 = (f32[4,32,1024]{2,1,0:T(8,128)S(1)}, f32[4,32,1024]{2,1,0:T(8,128)S(1)}, u32[]{:S(2)}, u32[]{:S(2)}) collective-permute-start(f32[4,32,1024]{2,1,0:T(8,128)S(1)} %pack.1.refs_0_), channel_id=1, source_target_pairs={{0,6},{2,4},{4,2},{6,0},{8,14},{10,12},{12,10},{14,8},{16,22},{18,... | collective-permute-start | bytes 1572872 | tf_op jit(solution)/shard_map/ppermute | solution.py:496
  18.7 33.2 %factor.3 = (bf16[1024,1024]{1,0:T(8,128)(2,1)S(1)}, bf16[1024,1024]{1,0:T(8,128)(2,1)S(1)}, f32[1024,128]{1,0:T(8,128)}, bf16[128,128]{1,0:T(8,128)(2,1)}, bf16...) custom-call(s32[1]{0:T(128)} %bitcast.1.core_ref, f32[512,1024]{1,0:T(8,128)} %own_ref.3, ...), custom_call_target="tpu_custom_call" | custom-call | flops 6442450944 | bytes 120000000 | tf_op jit(solution)/shard_map/factor/pallas_call | solution.py:280
  51.9 0.0 collective-permute-done.4.refs_1_
  51.9 0.0 collective-permute-done.5.refs_2_
  51.9 0.0 collective-permute-done.6.refs_3_
  51.9 0.0 copy-start.1
  51.9 0.0 copy-start.2
  52.0 0.0 copy-start.3
  52.0 3.3 %solve.1 = (f32[32,1024]{1,0:T(8,128)}, bf16[512,1024]{1,0:T(8,128)(2,1)S(1)}) custom-call(s32[1]{0:T(128)} %bitcast.blk_ref, bf16[1024,1024]{1,0:T(8,128)(2,1)S(1)} %get-tuple-element.19.high_ref, bf16[1024,1024]{1,0:T(8,128)(2,1)S(1)} %get-tuple-element.20.low_ref, f32[4,32,1024]{2,1,0:T(8,128)S(1)} %pack.1.refs_0_, ...), custom_call_target="tpu_custom_call" | custom-call | tf_op jit(solution)/shard_map/solve/pallas_call | solution.py:354
  55.2 2.1 %collective-permute-start.7 = (bf16[512,1024]{1,0:T(8,128)(2,1)S(1)}, bf16[512,1024]{1,0:T(8,128)(2,1)S(1)}, u32[]{:S(2)}, u32[]{:S(2)}) collective-permute-start(bf16[512,1024]{1,0:T(8,128)(2,1)S(1)} %get-tuple-element.22.mine_ref), channel_id=1, source_target_pairs={{0,1},{1,0},{2,3},{3,2},{4,5},{5,4},{6,7},{7,6},{8,9},{9,8},{10,11... | collective-permute-start | bytes 3145736 | tf_op jit(solution)/shard_map/ppermute | solution.py:510
  57.3 2.3 %collective-permute-done.7.theirs_ref = bf16[512,1024]{1,0:T(8,128)(2,1)S(1)} collective-permute-done((bf16[512,1024]{1,0:T(8,128)(2,1)S(1)}, bf16[512,1024]{1,0:T(8,128)(2,1)S(1)}, u32[]{:S(2)}, u32[]{:S(2)}) %collective-permute-start.7) | collective-permute-done | bytes 1048608 | tf_op jit(solution)/shard_map/ppermute | solution.py:510
  59.6 0.0 copy-done.1
  59.6 0.0 copy-done.2
  59.6 0.0 copy-done.3
  59.6 5.6 %update.1 = f32[6,8,128,256]{3,2,1,0:T(8,128)} custom-call(s32[1]{0:T(128)} %bitcast.1.core_ref, s32[4]{0:T(128)S(1)} %copy-done.2, s32[6]{0:T(128)S(1)} %copy-done.3, s32[6,8]{1,0:T(8,128)S(1)} %copy-done.1, bf16[512,1024]{1,0:T(8,128)(2,1)S(1)} %get-tuple-element.22.mine_ref, ...), custom_call_target="tpu_custom_call", output_to_operand_aliasing={{}: (7, {})} | custom-call | tf_op jit(solution)/shard_map/update/pallas_call | solution.py:465
  (1 shorter events, 0.0 us)
Async XLA Ops:
  0.6 4.9 %collective-permute-start = (f32[512,1024]{1,0:T(8,128)}, f32[512,1024]{1,0:T(8,128)}, u32[]{:S(2)}, u32[]{:S(2)}) collective-permute-start(f32[512,1024]{1,0:T(8,128)} %own_ref.3), channel_id=1, source_target_pairs={{0,1},{1,0},{2,3},{3,2},{4,5},{5,4},{6,7},{7,6},{8,9},{9,8},{10,11... | collective-permute-start | bytes 6291464 | tf_op jit(solution)/shard_map/ppermute | solution.py:493
  1.4 14.4 %collective-permute-start.1 = (f32[1,32,1024]{2,1,0:T(8,128)}, f32[1,32,1024]{2,1,0:T(8,128)S(1)}, u32[]{:S(2)}, u32[]{:S(2)}) collective-permute-start(f32[1,32,1024]{2,1,0:T(8,128)} %refs_0_.1), channel_id=1, source_target_pairs={{0,8},{2,10},{4,12},{6,14},{8,0},{10,2},{12,4},{14,6},{16,24},{18,... | collective-permute-start | bytes 393224 | tf_op jit(solution)/shard_map/ppermute | solution.py:496
  2.7 13.1 %collective-permute-start.2 = (f32[1,32,1024]{2,1,0:T(8,128)}, f32[1,32,1024]{2,1,0:T(8,128)S(1)}, u32[]{:S(2)}, u32[]{:S(2)}) collective-permute-start(f32[1,32,1024]{2,1,0:T(8,128)} %refs_0_.1), channel_id=1, source_target_pairs={{0,16},{2,18},{4,20},{6,22},{8,24},{10,26},{12,28},{14,30},{16,0},... | collective-permute-start | bytes 393224 | tf_op jit(solution)/shard_map/ppermute | solution.py:496
  2.7 13.2 %collective-permute-start.3 = (f32[1,32,1024]{2,1,0:T(8,128)}, f32[1,32,1024]{2,1,0:T(8,128)S(1)}, u32[]{:S(2)}, u32[]{:S(2)}) collective-permute-start(f32[1,32,1024]{2,1,0:T(8,128)} %refs_0_.1), channel_id=1, source_target_pairs={{0,24},{2,26},{4,28},{6,30},{8,16},{10,18},{12,20},{14,22},{16,8},... | collective-permute-start | bytes 393224 | tf_op jit(solution)/shard_map/ppermute | solution.py:496
  5.5 10.5 %copy-start = (f32[1,32,1024]{2,1,0:T(8,128)S(1)}, f32[1,32,1024]{2,1,0:T(8,128)}, u32[]{:S(2)}) copy-start(f32[1,32,1024]{2,1,0:T(8,128)} %refs_0_.1) | copy-start | bytes 393220
  16.0 35.9 %collective-permute-start.4 = (f32[4,32,1024]{2,1,0:T(8,128)S(1)}, f32[4,32,1024]{2,1,0:T(8,128)S(1)}, u32[]{:S(2)}, u32[]{:S(2)}) collective-permute-start(f32[4,32,1024]{2,1,0:T(8,128)S(1)} %pack.1.refs_0_), channel_id=1, source_target_pairs={{0,2},{2,0},{4,6},{6,4},{8,10},{10,8},{12,14},{14,12},{16,18},{18,... | collective-permute-start | bytes 1572872 | tf_op jit(solution)/shard_map/ppermute | solution.py:496
  16.3 35.6 %collective-permute-start.5 = (f32[4,32,1024]{2,1,0:T(8,128)S(1)}, f32[4,32,1024]{2,1,0:T(8,128)S(1)}, u32[]{:S(2)}, u32[]{:S(2)}) collective-permute-start(f32[4,32,1024]{2,1,0:T(8,128)S(1)} %pack.1.refs_0_), channel_id=1, source_target_pairs={{0,4},{2,6},{4,0},{6,2},{8,12},{10,14},{12,8},{14,10},{16,20},{18,... | collective-permute-start | bytes 1572872 | tf_op jit(solution)/shard_map/ppermute | solution.py:496
  16.6 35.4 %collective-permute-start.6 = (f32[4,32,1024]{2,1,0:T(8,128)S(1)}, f32[4,32,1024]{2,1,0:T(8,128)S(1)}, u32[]{:S(2)}, u32[]{:S(2)}) collective-permute-start(f32[4,32,1024]{2,1,0:T(8,128)S(1)} %pack.1.refs_0_), channel_id=1, source_target_pairs={{0,6},{2,4},{4,2},{6,0},{8,14},{10,12},{12,10},{14,8},{16,22},{18,... | collective-permute-start | bytes 1572872 | tf_op jit(solution)/shard_map/ppermute | solution.py:496
  51.9 7.7 %copy-start.1 = (s32[6,8]{1,0:T(8,128)S(1)}, s32[6,8]{1,0:T(8,128)}, u32[]{:S(2)}) copy-start(s32[6,8]{1,0:T(8,128)} %block_rows_ref.1) | copy-start | bytes 580
  51.9 7.7 %copy-start.2 = (s32[4]{0:T(128)S(1)}, s32[4]{0:T(128)}, u32[]{:S(2)}) copy-start(s32[4]{0:T(128)} %row_ids_ref.1) | copy-start | bytes 52
  52.0 7.7 %copy-start.3 = (s32[6]{0:T(128)S(1)}, s32[6]{0:T(128)}, u32[]{:S(2)}) copy-start(s32[6]{0:T(128)} %col_ids_ref.1) | copy-start | bytes 76
  55.2 4.4 %collective-permute-start.7 = (bf16[512,1024]{1,0:T(8,128)(2,1)S(1)}, bf16[512,1024]{1,0:T(8,128)(2,1)S(1)}, u32[]{:S(2)}, u32[]{:S(2)}) collective-permute-start(bf16[512,1024]{1,0:T(8,128)(2,1)S(1)} %get-tuple-element.22.mine_ref), channel_id=1, source_target_pairs={{0,1},{1,0},{2,3},{3,2},{4,5},{5,4},{6,7},{7,6},{8,9},{9,8},{10,11... | collective-permute-start | bytes 3145736 | tf_op jit(solution)/shard_map/ppermute | solution.py:510
where the time goes:
time: 64.7 us; the launch traced here: 65.2 us
  Pallas kernels  52.3 us (81%)
  starting transfers between devices  8.2 us (13%)
  waiting for transfers between devices  4 us (6%)
  between operations  0.73 us (1%)
    pallas_call x2, Pallas kernels, factor(): pl.pallas_call(functools.partial(factor_kernel, first, last), out_shape=o...  43.4 us
    pallas_call x1, Pallas kernels, update(): pl.pallas_call(update_kernel, out_shape=jax.ShapeDtypeStruct(blocks.shape...  5.61 us
    ppermute x6, starting transfers between devices, from_partner(): return lax.ppermute(value, 'blk', [(i, i ^ k) for i in range(n_blk)])  5.38 us
    pallas_call x1, Pallas kernels, solve(): pl.pallas_call(solve_kernel, out_shape=[jax.ShapeDtypeStruct((part, order...  3.25 us
    ppermute x1, waiting for transfers between devices, local(): theirs = lax.ppermute(mine, 'row', swap)  2.29 us
    ppermute x1, starting transfers between devices, local(): theirs = lax.ppermute(mine, 'row', swap)  2.09 us
    ppermute x1, waiting for transfers between devices, local(): other = lax.ppermute(diag_block, 'row', swap)  1.46 us
  transfers between devices with their start and end apart: 8, of which 3 were waited for; matrix products, arithmetic and copies ran while one was open for 0% of the time, Pallas kernels for 67%

commit v1 on v0

--- a/solution.py
+++ b/solution.py
@@ -139,7 +139,8 @@
     high_ref, low_ref, base, prev_high, prev_low, diag = refs[:6]
     refs = refs[6:]
     copied_ref = refs.pop(0) if first else None
-    matrix, unit, scratch_diag, scratch_below, scratch_rows, tile_sems = refs[:6]
+    matrix, unit, next_diag, column_high, column_low = refs[:5]
+    scratch_diag, scratch_below, scratch_rows, tile_sems = refs[5:9]
     order = own_ref.shape[1]
     half = order // 2
     count = order // BLOCK
@@ -158,7 +159,7 @@
         for which in range(2):
             fetch_tile(t, which).start()
     if first:
-        held, block_sems = refs[6:]
+        held, block_sems = refs[9:]
         fetch_blocks = pltpu.make_async_copy(blocks_ref, held, block_sems.at[0])
         store_blocks = pltpu.make_async_copy(held, copied_ref, block_sems.at[1])
         fetch_blocks.start()
@@ -167,6 +168,7 @@
         == lax.broadcasted_iota(jnp.int32, (BLOCK, BLOCK), 1)
     ).astype(F32)
     row_at = lax.broadcasted_iota(jnp.int32, (order, BLOCK), 0)
+    lane_at = lax.broadcasted_iota(jnp.int32, (order, BLOCK), 1)
 
     if first:
         done = (first - 1) * BLOCK
@@ -185,17 +187,12 @@
             fetch_tile(0, which).wait()
         diag[...] = matrix[0, :BLOCK, :]
 
-    def store_previous(b):
-        before = pl.multiple_of(jnp.maximum(b - 1, 0) * BLOCK, BLOCK)
-        high_ref[pl.ds(before, BLOCK), :] = jnp.zeros((BLOCK, width), BF16)
-        low_ref[pl.ds(before, BLOCK), :] = jnp.zeros((BLOCK, width), BF16)
-        column = times_transposed(*halves(base[...]), prev_high[...], prev_low[...])
-        high, low = halves(column)
-        high_ref[:, pl.ds(before, BLOCK)] = high
-        low_ref[:, pl.ds(before, BLOCK)] = low
+    def previous_column():
+        return halves(times_transposed(*halves(base[...]), prev_high[...], prev_low[...]))
 
     def block_step(b, carry):
         here = pl.multiple_of(b * BLOCK, BLOCK)
+        before = pl.multiple_of(jnp.maximum(b - 1, 0) * BLOCK, BLOCK)
         following = jnp.minimum(b + 1, count - 1)
         next_at = pl.multiple_of(following * BLOCK, BLOCK)
 
@@ -211,18 +208,23 @@
                 fetch_blocks.wait()
                 store_blocks.start()
 
-        store_previous(b)
-        earlier = times_transposed(
-            high_ref[...],
-            low_ref[...],
-            high_ref[pl.ds(here, BLOCK), :],
-            low_ref[pl.ds(here, BLOCK), :],
-        )
-        base[...] = jnp.where(row_at >= here, matrix[b], 0.0) - earlier
-        base[pl.ds(here, BLOCK), :] = identity
-        next_high, next_low = high_ref[pl.ds(next_at, BLOCK), :], low_ref[pl.ds(next_at, BLOCK), :]
-        next_diag = matrix[following, pl.ds(next_at, BLOCK), :] - times_transposed(
-            next_high, next_low, next_high, next_low
+        column_high[...], column_low[...] = previous_column()
+
+        def rows_of(at):
+            rows = pl.ds(at, BLOCK)
+            return (high_ref[rows, :], low_ref[rows, :]), (column_high[rows, :], column_low[rows, :])
+
+        history, column = rows_of(here)
+        earlier = times_transposed(high_ref[...], low_ref[...], *history)
+        earlier += times_transposed(column_high[...], column_low[...], *column)
+        fresh = jnp.where(row_at >= here, matrix[b], 0.0) - earlier
+        in_diag = (row_at >= here) & (row_at < here + BLOCK)
+        base[...] = jnp.where(in_diag, (row_at - here == lane_at).astype(F32), fresh)
+        history, column = rows_of(next_at)
+        next_diag[...] = (
+            matrix[following, pl.ds(next_at, BLOCK), :]
+            - times_transposed(*history, *history)
+            - times_transposed(*column, *column)
         )
 
         unit[...] = identity
@@ -233,12 +235,16 @@
         prev_low[...] = low
         below = times_transposed(*halves(base[pl.ds(next_at, BLOCK), :]), high, low)
         high, low = halves(below)
-        diag[...] = next_diag - times_transposed(high, low, high, low)
+        diag[...] = next_diag[...] - times_transposed(high, low, high, low)
+
+        for ref, column in ((high_ref, column_high), (low_ref, column_low)):
+            ref[:, pl.ds(before, BLOCK)] = column[...]
+            ref[pl.ds(here, BLOCK), :] = jnp.zeros((BLOCK, width), BF16)
         return carry
 
     lax.fori_loop(first, last, block_step, 0)
     if last == count:
-        store_previous(count)
+        high_ref[:, order - BLOCK :], low_ref[:, order - BLOCK :] = previous_column()
     if first:
         store_blocks.wait()
 
@@ -260,6 +266,9 @@
     scratch = [
         pltpu.VMEM((count, order, BLOCK), F32),
         pltpu.VMEM((BLOCK, BLOCK), F32),
+        pltpu.VMEM((BLOCK, BLOCK), F32),
+        pltpu.VMEM((order, BLOCK), BF16),
+        pltpu.VMEM((order, BLOCK), BF16),
         pltpu.VMEM((PANEL // STEP, STEP, STEP, BLOCK), F32),
         pltpu.VMEM((PANEL // STEP, STEP, PANEL - STEP, BLOCK), F32),
         pltpu.VMEM((PANEL // STEP, 2, 2, STEP, BLOCK), F32),

time: 64.7 us -> 67.1 us (1.037)
  the two profiles are of different devices: /device:TPU:23 before, /device:TPU:3 now
where the time goes in v1:
time: 67.1 us; the launch traced here: 65.8 us
  Pallas kernels  53.9 us (80%)
  starting transfers between devices  8.36 us (12%)
  waiting for transfers between devices  2.81 us (4%)
  between operations  0.75 us (1%)
    pallas_call x2, Pallas kernels, factor(): pl.pallas_call(functools.partial(factor_kernel, first, last), out_shape=o...  47 us
    ppermute x6, starting transfers between devices, from_partner(): return lax.ppermute(value, 'blk', [(i, i ^ k) for i in range(n_blk)])  6.33 us
    pallas_call x1, Pallas kernels, update(): pl.pallas_call(update_kernel, out_shape=jax.ShapeDtypeStruct(blocks.shape...  3.56 us
    pallas_call x1, Pallas kernels, solve(): pl.pallas_call(solve_kernel, out_shape=[jax.ShapeDtypeStruct((part, order...  3.25 us
    ppermute x1, waiting for transfers between devices, local(): theirs = lax.ppermute(mine, 'row', swap)  2.29 us
  transfers between devices with their start and end apart: 8, of which 2 were waited for; matrix products, arithmetic and copies ran while one was open for 0% of the time, Pallas kernels for 71%

profile of v1, /device:TPU:3, one launch (start us, length us, event | category | flops | bytes accessed | tf_op | source)
XLA Modules:
  0.0 65.8 jit_solution(798889200559161861)
XLA Ops:
  0.6 0.7 %collective-permute-start = (f32[512,1024]{1,0:T(8,128)}, f32[512,1024]{1,0:T(8,128)}, u32[]{:S(2)}, u32[]{:S(2)}) collective-permute-start(f32[512,1024]{1,0:T(8,128)} %own_ref.3), channel_id=1, source_target_pairs={{0,1},{1,0},{2,3},{3,2},{4,5},{5,4},{6,7},{7,6},{8,9},{9,8},{10,11... | collective-permute-start | bytes 6291464 | tf_op jit(solution)/shard_map/ppermute | solution.py:502
  1.4 1.3 %collective-permute-start.1 = (f32[1,32,1024]{2,1,0:T(8,128)}, f32[1,32,1024]{2,1,0:T(8,128)S(1)}, u32[]{:S(2)}, u32[]{:S(2)}) collective-permute-start(f32[1,32,1024]{2,1,0:T(8,128)} %refs_0_.1), channel_id=1, source_target_pairs={{0,8},{2,10},{4,12},{6,14},{8,0},{10,2},{12,4},{14,6},{16,24},{18,... | collective-permute-start | bytes 393224 | tf_op jit(solution)/shard_map/ppermute | solution.py:505
  2.7 2.3 %collective-permute-start.2 = (f32[1,32,1024]{2,1,0:T(8,128)}, f32[1,32,1024]{2,1,0:T(8,128)S(1)}, u32[]{:S(2)}, u32[]{:S(2)}) collective-permute-start(f32[1,32,1024]{2,1,0:T(8,128)} %refs_0_.1), channel_id=1, source_target_pairs={{0,16},{2,18},{4,20},{6,22},{8,24},{10,26},{12,28},{14,30},{16,0},... | collective-permute-start | bytes 393224 | tf_op jit(solution)/shard_map/ppermute | solution.py:505
  5.0 0.0 collective-permute-start.3
  5.0 0.5 collective-permute-done.other_ref
  5.5 0.0 copy-start
  5.5 10.5 %factor.2 = (bf16[1024,128]{1,0:T(8,128)(2,1)S(1)}, bf16[1024,128]{1,0:T(8,128)(2,1)S(1)}, f32[1024,128]{1,0:T(8,128)S(1)}, bf16[128,128]{1,0:T(8,128)(2,1)S(1)}...) custom-call(s32[1]{0:T(128)} %bitcast.1.core_ref, f32[512,1024]{1,0:T(8,128)} %own_ref.3, ...), custom_call_target="tpu_custom_call" | custom-call | flops 2147483648 | bytes 40000000 | tf_op jit(solution)/shard_map/factor/pallas_call | solution.py:289
  16.0 0.0 collective-permute-done.1.refs_1_
  16.0 0.0 collective-permute-done.2.refs_2_
  16.0 0.0 collective-permute-done.3.refs_3_
  16.0 0.0 copy-done
  16.1 0.1 collective-permute-start.4
  16.1 1.5 %collective-permute-start.5 = (f32[4,32,1024]{2,1,0:T(8,128)S(1)}, f32[4,32,1024]{2,1,0:T(8,128)S(1)}, u32[]{:S(2)}, u32[]{:S(2)}) collective-permute-start(f32[4,32,1024]{2,1,0:T(8,128)S(1)} %pack.1.refs_0_), channel_id=1, source_target_pairs={{0,4},{2,6},{4,0},{6,2},{8,12},{10,14},{12,8},{14,10},{16,20},{18,... | collective-permute-start | bytes 1572872 | tf_op jit(solution)/shard_map/ppermute | solution.py:505
  17.6 1.2 %collective-permute-start.6 = (f32[4,32,1024]{2,1,0:T(8,128)S(1)}, f32[4,32,1024]{2,1,0:T(8,128)S(1)}, u32[]{:S(2)}, u32[]{:S(2)}) collective-permute-start(f32[4,32,1024]{2,1,0:T(8,128)S(1)} %pack.1.refs_0_), channel_id=1, source_target_pairs={{0,6},{2,4},{4,2},{6,0},{8,14},{10,12},{12,10},{14,8},{16,22},{18,... | collective-permute-start | bytes 1572872 | tf_op jit(solution)/shard_map/ppermute | solution.py:505
  18.8 36.6 %factor.3 = (bf16[1024,1024]{1,0:T(8,128)(2,1)S(1)}, bf16[1024,1024]{1,0:T(8,128)(2,1)S(1)}, f32[1024,128]{1,0:T(8,128)}, bf16[128,128]{1,0:T(8,128)(2,1)}, bf16...) custom-call(s32[1]{0:T(128)} %bitcast.1.core_ref, f32[512,1024]{1,0:T(8,128)} %own_ref.3, ...), custom_call_target="tpu_custom_call" | custom-call | flops 6442450944 | bytes 120000000 | tf_op jit(solution)/shard_map/factor/pallas_call | solution.py:289
  55.4 0.0 collective-permute-done.4.refs_1_
  55.4 0.0 collective-permute-done.5.refs_2_
  55.4 0.0 collective-permute-done.6.refs_3_
  55.4 0.0 copy-start.1
  55.4 0.0 copy-start.2
  55.4 0.0 copy-start.3
  55.4 3.2 %solve.1 = (f32[32,1024]{1,0:T(8,128)}, bf16[512,1024]{1,0:T(8,128)(2,1)S(1)}) custom-call(s32[1]{0:T(128)} %bitcast.blk_ref, bf16[1024,1024]{1,0:T(8,128)(2,1)S(1)} %get-tuple-element.19.high_ref, bf16[1024,1024]{1,0:T(8,128)(2,1)S(1)} %get-tuple-element.20.low_ref, f32[4,32,1024]{2,1,0:T(8,128)S(1)} %pack.1.refs_0_, ...), custom_call_target="tpu_custom_call" | custom-call | tf_op jit(solution)/shard_map/solve/pallas_call | solution.py:363
  58.7 1.3 %collective-permute-start.7 = (bf16[512,1024]{1,0:T(8,128)(2,1)S(1)}, bf16[512,1024]{1,0:T(8,128)(2,1)S(1)}, u32[]{:S(2)}, u32[]{:S(2)}) collective-permute-start(bf16[512,1024]{1,0:T(8,128)(2,1)S(1)} %get-tuple-element.22.mine_ref), channel_id=1, source_target_pairs={{0,1},{1,0},{2,3},{3,2},{4,5},{5,4},{6,7},{7,6},{8,9},{9,8},{10,11... | collective-permute-start | bytes 3145736 | tf_op jit(solution)/shard_map/ppermute | solution.py:519
  60.0 2.3 %collective-permute-done.7.theirs_ref = bf16[512,1024]{1,0:T(8,128)(2,1)S(1)} collective-permute-done((bf16[512,1024]{1,0:T(8,128)(2,1)S(1)}, bf16[512,1024]{1,0:T(8,128)(2,1)S(1)}, u32[]{:S(2)}, u32[]{:S(2)}) %collective-permute-start.7) | collective-permute-done | bytes 1048608 | tf_op jit(solution)/shard_map/ppermute | solution.py:519
  62.3 0.0 copy-done.1
  62.3 0.0 copy-done.2
  62.3 0.0 copy-done.3
  62.3 3.6 %update.1 = f32[6,8,128,256]{3,2,1,0:T(8,128)} custom-call(s32[1]{0:T(128)} %bitcast.1.core_ref, s32[4]{0:T(128)S(1)} %copy-done.2, s32[6]{0:T(128)S(1)} %copy-done.3, s32[6,8]{1,0:T(8,128)S(1)} %copy-done.1, bf16[512,1024]{1,0:T(8,128)(2,1)S(1)} %get-tuple-element.22.mine_ref, ...), custom_call_target="tpu_custom_call", output_to_operand_aliasing={{}: (7, {})} | custom-call | tf_op jit(solution)/shard_map/update/pallas_call | solution.py:474
  (1 shorter events, 0.0 us)
Async XLA Ops:
  0.6 4.9 %collective-permute-start = (f32[512,1024]{1,0:T(8,128)}, f32[512,1024]{1,0:T(8,128)}, u32[]{:S(2)}, u32[]{:S(2)}) collective-permute-start(f32[512,1024]{1,0:T(8,128)} %own_ref.3), channel_id=1, source_target_pairs={{0,1},{1,0},{2,3},{3,2},{4,5},{5,4},{6,7},{7,6},{8,9},{9,8},{10,11... | collective-permute-start | bytes 6291464 | tf_op jit(solution)/shard_map/ppermute | solution.py:502
  1.4 14.6 %collective-permute-start.1 = (f32[1,32,1024]{2,1,0:T(8,128)}, f32[1,32,1024]{2,1,0:T(8,128)S(1)}, u32[]{:S(2)}, u32[]{:S(2)}) collective-permute-start(f32[1,32,1024]{2,1,0:T(8,128)} %refs_0_.1), channel_id=1, source_target_pairs={{0,8},{2,10},{4,12},{6,14},{8,0},{10,2},{12,4},{14,6},{16,24},{18,... | collective-permute-start | bytes 393224 | tf_op jit(solution)/shard_map/ppermute | solution.py:505
  2.7 13.3 %collective-permute-start.2 = (f32[1,32,1024]{2,1,0:T(8,128)}, f32[1,32,1024]{2,1,0:T(8,128)S(1)}, u32[]{:S(2)}, u32[]{:S(2)}) collective-permute-start(f32[1,32,1024]{2,1,0:T(8,128)} %refs_0_.1), channel_id=1, source_target_pairs={{0,16},{2,18},{4,20},{6,22},{8,24},{10,26},{12,28},{14,30},{16,0},... | collective-permute-start | bytes 393224 | tf_op jit(solution)/shard_map/ppermute | solution.py:505
  5.0 11.0 %collective-permute-start.3 = (f32[1,32,1024]{2,1,0:T(8,128)}, f32[1,32,1024]{2,1,0:T(8,128)S(1)}, u32[]{:S(2)}, u32[]{:S(2)}) collective-permute-start(f32[1,32,1024]{2,1,0:T(8,128)} %refs_0_.1), channel_id=1, source_target_pairs={{0,24},{2,26},{4,28},{6,30},{8,16},{10,18},{12,20},{14,22},{16,8},... | collective-permute-start | bytes 393224 | tf_op jit(solution)/shard_map/ppermute | solution.py:505
  5.5 10.5 %copy-start = (f32[1,32,1024]{2,1,0:T(8,128)S(1)}, f32[1,32,1024]{2,1,0:T(8,128)}, u32[]{:S(2)}) copy-start(f32[1,32,1024]{2,1,0:T(8,128)} %refs_0_.1) | copy-start | bytes 393220
  16.1 39.3 %collective-permute-start.4 = (f32[4,32,1024]{2,1,0:T(8,128)S(1)}, f32[4,32,1024]{2,1,0:T(8,128)S(1)}, u32[]{:S(2)}, u32[]{:S(2)}) collective-permute-start(f32[4,32,1024]{2,1,0:T(8,128)S(1)} %pack.1.refs_0_), channel_id=1, source_target_pairs={{0,2},{2,0},{4,6},{6,4},{8,10},{10,8},{12,14},{14,12},{16,18},{18,... | collective-permute-start | bytes 1572872 | tf_op jit(solution)/shard_map/ppermute | solution.py:505
  16.1 39.2 %collective-permute-start.5 = (f32[4,32,1024]{2,1,0:T(8,128)S(1)}, f32[4,32,1024]{2,1,0:T(8,128)S(1)}, u32[]{:S(2)}, u32[]{:S(2)}) collective-permute-start(f32[4,32,1024]{2,1,0:T(8,128)S(1)} %pack.1.refs_0_), channel_id=1, source_target_pairs={{0,4},{2,6},{4,0},{6,2},{8,12},{10,14},{12,8},{14,10},{16,20},{18,... | collective-permute-start | bytes 1572872 | tf_op jit(solution)/shard_map/ppermute | solution.py:505
  17.6 37.8 %collective-permute-start.6 = (f32[4,32,1024]{2,1,0:T(8,128)S(1)}, f32[4,32,1024]{2,1,0:T(8,128)S(1)}, u32[]{:S(2)}, u32[]{:S(2)}) collective-permute-start(f32[4,32,1024]{2,1,0:T(8,128)S(1)} %pack.1.refs_0_), channel_id=1, source_target_pairs={{0,6},{2,4},{4,2},{6,0},{8,14},{10,12},{12,10},{14,8},{16,22},{18,... | collective-permute-start | bytes 1572872 | tf_op jit(solution)/shard_map/ppermute | solution.py:505
  55.4 6.9 %copy-start.1 = (s32[6,8]{1,0:T(8,128)S(1)}, s32[6,8]{1,0:T(8,128)}, u32[]{:S(2)}) copy-start(s32[6,8]{1,0:T(8,128)} %block_rows_ref.1) | copy-start | bytes 580
  55.4 6.9 %copy-start.2 = (s32[4]{0:T(128)S(1)}, s32[4]{0:T(128)}, u32[]{:S(2)}) copy-start(s32[4]{0:T(128)} %row_ids_ref.1) | copy-start | bytes 52
  55.4 6.9 %copy-start.3 = (s32[6]{0:T(128)S(1)}, s32[6]{0:T(128)}, u32[]{:S(2)}) copy-start(s32[6]{0:T(128)} %col_ids_ref.1) | copy-start | bytes 76
  58.7 3.6 %collective-permute-start.7 = (bf16[512,1024]{1,0:T(8,128)(2,1)S(1)}, bf16[512,1024]{1,0:T(8,128)(2,1)S(1)}, u32[]{:S(2)}, u32[]{:S(2)}) collective-permute-start(bf16[512,1024]{1,0:T(8,128)(2,1)S(1)} %get-tuple-element.22.mine_ref), channel_id=1, source_target_pairs={{0,1},{1,0},{2,3},{3,2},{4,5},{5,4},{6,7},{7,6},{8,9},{9,8},{10,11... | collective-permute-start | bytes 3145736 | tf_op jit(solution)/shard_map/ppermute | solution.py:519
